TPU v7x, 32 devices: a whole 2x2x4 slice. The times are simulated.
32 devices in a mesh: groups: 2 (over y), wide: 8 (over z, x), narrow: 2 (over core).
Axes of the slice: x: 2, y: 2, z: 4, core: 2. Of those that a mesh axis runs over, the one named last changes fastest.
Arguments:
- inputs: bfloat16 [8192, 1024], P(('groups', 'wide', 'narrow')), parts along dimension 0, may hold values from -6 to 6
- filter_taps: bfloat16 [4096, 1024], P(('wide', 'narrow')), may hold values from -6 to 6
- grad_out: bfloat16 [8192, 1024], P(('groups', 'wide', 'narrow')), parts along dimension 0, may hold values from -6 to 6
Outputs:
- outputs: bfloat16 [8192, 1024], P(('groups', 'wide', 'narrow')), parts along dimension 0
- grad_inputs: bfloat16 [8192, 1024], P(('groups', 'wide', 'narrow')), parts along dimension 0
- grad_taps: bfloat16 [8192, 1024], P(('groups', 'wide', 'narrow')), parts along dimension 0
There are 2 independent parts, one for each index of `groups`. A program takes and returns all parts, laid end to end along the dimension named above; an argument that names none is the same for every part. Nothing has to cross between parts.
All inputs are finite; a program needn't handle non-finite values.
Results may differ from a plain program's by a relative error of at most 0.008.
Values may be sent and summed in bfloat16 or wider, within the bound.
A program may use at most 64 MiB of HBM per device.

v0:
```python
import math
import jax
import jax.numpy as jnp
from jax import lax
from jax.sharding import PartitionSpec as P


def partner_2(value, axis, distance):
    mask = 2**distance
    pairs = [(source, source ^ mask) for source in range(lax.axis_size(axis))]
    return lax.ppermute(value, axis, pairs)


def on_device(inputs, filter_taps, grad_out):
    span_count = lax.axis_size("wide")
    blocksize = inputs.shape[0]
    channels = inputs.shape[1]
    shares = channels // span_count
    row_count = span_count * shares
    seq_len = span_count * 2 * blocksize
    parity = lax.axis_index("narrow")
    signed = (1 - 2 * parity).astype(jnp.float32)
    counter = jnp.arange(span_count, dtype=jnp.int32)
    long_angles = (counter[:, None] * counter[None, :] % span_count).astype(jnp.float32) * (
        2.0 * math.pi / span_count
    )
    long_cos = jnp.cos(long_angles)
    long_sin = jnp.sin(long_angles)
    long_forward = jnp.concatenate([long_cos, -long_sin], axis=0).astype(jnp.bfloat16)
    long_inverse = jnp.concatenate([long_cos, -long_sin], axis=1).astype(jnp.bfloat16)
    positions = jnp.arange(blocksize, dtype=jnp.int32)

    def first_section(pieces, twist_cos, twist_sin):
        share_count = pieces.shape[1]
        lane_count = pieces.shape[2]
        flatten = pieces.reshape(span_count, share_count * lane_count)
        mixture = jnp.dot(long_forward, flatten, preferred_element_type=jnp.float32)
        mixture = mixture.reshape(2, span_count, share_count, lane_count)
        real_part = mixture[0] * twist_cos + mixture[1] * twist_sin
        imag_part = mixture[1] * twist_cos - mixture[0] * twist_sin
        return jnp.stack([real_part, imag_part]).astype(jnp.bfloat16)

    def long_back(combined_re, combined_im, twist_cos, twist_sin):
        merged_re = combined_re * twist_cos - combined_im * twist_sin
        merged_im = combined_im * twist_cos + combined_re * twist_sin
        share_count = combined_re.shape[1]
        lane_count = combined_re.shape[2]
        stacked = (
            jnp.stack([merged_re, merged_im])
            .astype(jnp.bfloat16)
            .reshape(2 * span_count, share_count * lane_count)
        )
        summed = jnp.dot(long_inverse, stacked, preferred_element_type=jnp.float32) * (
            1.0 / seq_len
        )
        return summed.astype(jnp.bfloat16).reshape(span_count, share_count, lane_count)

    block_product = positions[:, None] * (2 * positions[None, :] + parity) % (2 * blocksize)
    block_angles = block_product.astype(jnp.float32) * (math.pi / blocksize)
    block_cos = jnp.cos(block_angles)
    block_sin = jnp.sin(block_angles)
    forward_mat = jnp.concatenate(
        [
            jnp.concatenate([block_cos, -block_sin], axis=1),
            jnp.concatenate([block_sin, block_cos], axis=1),
        ],
        axis=0,
    ).astype(jnp.bfloat16)
    cos_turned = jnp.transpose(block_cos)
    sin_turned = jnp.transpose(block_sin)
    inverse_mat = jnp.concatenate(
        [
            jnp.concatenate([cos_turned, sin_turned], axis=1),
            jnp.concatenate([-sin_turned, cos_turned], axis=1),
        ],
        axis=0,
    ).astype(jnp.bfloat16)
    twist_product = (parity * blocksize + positions)[None, None, :] * counter[:, None, None]
    twist_angles = twist_product.astype(jnp.float32) * (2.0 * math.pi / seq_len)
    twist_cos = jnp.cos(twist_angles)
    twist_sin = jnp.sin(twist_angles)

    def section_pairs(pieces):
        return first_section(pieces, twist_cos, twist_sin)

    def spectrum(signal):
        arranged = jnp.transpose(signal).reshape(span_count, shares, blocksize)
        twisted = section_pairs(
            lax.all_to_all(arranged, "wide", split_axis=0, concat_axis=0, tiled=True)
        )
        partner = partner_2(twisted, "narrow", 0)
        paired = (signed * twisted.astype(jnp.float32) + partner.astype(jnp.float32)).astype(
            jnp.bfloat16
        )
        joined = jnp.concatenate(
            [paired[0].reshape(row_count, blocksize), paired[1].reshape(row_count, blocksize)],
            axis=1,
        )
        return jnp.dot(joined, forward_mat, preferred_element_type=jnp.float32)

    def invert(spectrum_in):
        unfolded = jnp.dot(spectrum_in, inverse_mat, preferred_element_type=jnp.float32).astype(
            jnp.bfloat16
        )
        partner = partner_2(unfolded, "narrow", 0)
        combined = signed * unfolded.astype(jnp.float32) + partner.astype(jnp.float32)
        comb_re = combined[:, :blocksize].reshape(span_count, shares, blocksize)
        comb_im = combined[:, blocksize:].reshape(span_count, shares, blocksize)
        arranged = long_back(comb_re, comb_im, twist_cos, twist_sin)
        returned = lax.all_to_all(arranged, "wide", split_axis=0, concat_axis=1, tiled=True)
        return jnp.transpose(returned.reshape(channels, blocksize))

    def product(left_side, right_side, conjugate, factor):
        left_re = left_side[..., :blocksize]
        left_im = left_side[..., blocksize:]
        right_re = right_side[..., :blocksize]
        right_im = right_side[..., blocksize:]
        if conjugate:
            real_part = left_re * right_re + left_im * right_im
            imag_part = left_re * right_im - left_im * right_re
        else:
            real_part = left_re * right_re - left_im * right_im
            imag_part = left_re * right_im + left_im * right_re
        return (jnp.concatenate([real_part, imag_part], axis=-1) * factor).astype(jnp.bfloat16)

    kernel_scale = 1.0 / math.sqrt(seq_len)
    input_spectrum = spectrum(inputs)
    kernel_spectrum = spectrum(filter_taps) * kernel_scale
    outputs = invert(product(kernel_spectrum, input_spectrum, False, 1.0))
    grad_spectrum = spectrum(grad_out)
    grad_inputs = invert(product(kernel_spectrum, grad_spectrum, True, 1.0))
    grad_taps = invert(product(input_spectrum, grad_spectrum, True, kernel_scale))
    return (outputs, grad_inputs, grad_taps)


def solution(mesh):
    in_specs = (
        P(("groups", "wide", "narrow"), None),
        P(("wide", "narrow"), None),
        P(("groups", "wide", "narrow"), None),
    )
    out_specs = (
        P(("groups", "wide", "narrow"), None),
        P(("groups", "wide", "narrow"), None),
        P(("groups", "wide", "narrow"), None),
    )
    return jax.shard_map(
        on_device, mesh=mesh, in_specs=in_specs, out_specs=out_specs, check_vma=False
    )
```

profile of v0, /device:TPU:0, one launch (start us, length us, event | category | flops | bytes accessed | tf_op | source)
XLA Modules:
  0.0 144.9 jit_solution(16948435035127631216)
XLA Ops:
  0.7 2.1 %copy.61 = bf16[1024,256]{1,0:T(8,128)(2,1)} copy(bf16[1024,256]{0,1:T(8,128)(2,1)} %bitcast.84) | data formatting | bytes 1048576 | tf_op jit(solution)/shard_map/reshape | solution.py:87
  2.8 7.3 %all-to-all-start.1 = ((bf16[8,128,256]{2,1,0:T(8,128)(2,1)}), bf16[8,128,256]{2,1,0:T(8,128)(2,1)S(1)}, u32[]{:S(2)}, u32[]{:S(2)}) async-start(bf16[8,128,256]{2,1,0:T(8,128)(2,1)} %bitcast.7), calls=%async_computation.1 | async-start | bytes 1048576 | tf_op jit(solution)/shard_map/all_to_all | solution.py:89
  11.0 13.5 %all-to-all-done.1 = bf16[8,128,256]{2,1,0:T(8,128)(2,1)S(1)} async-done(((bf16[8,128,256]{2,1,0:T(8,128)(2,1)}), bf16[8,128,256]{2,1,0:T(8,128)(2,1)S(1)}, u32[]{:S(2)}, u32[]{:S(2)}) %all-to-all-start.1) | async-done | bytes 524320 | tf_op jit(solution)/shard_map/all_to_all | solution.py:89
  24.5 3.6 %all-to-all-start = ((bf16[8,128,256]{2,1,0:T(8,128)(2,1)}), bf16[8,128,256]{2,1,0:T(8,128)(2,1)S(1)}, u32[]{:S(2)}, u32[]{:S(2)}) async-start(bf16[8,128,256]{2,1,0:T(8,128)(2,1)} %bitcast.1), calls=%async_computation | async-start | bytes 1048576 | tf_op jit(solution)/shard_map/all_to_all | solution.py:89
  29.2 13.7 %all-to-all-done = bf16[8,128,256]{2,1,0:T(8,128)(2,1)S(1)} async-done(((bf16[8,128,256]{2,1,0:T(8,128)(2,1)}), bf16[8,128,256]{2,1,0:T(8,128)(2,1)S(1)}, u32[]{:S(2)}, u32[]{:S(2)}) %all-to-all-start) | async-done | bytes 524320 | tf_op jit(solution)/shard_map/all_to_all | solution.py:89
  42.8 3.6 %all-to-all-start.3 = ((bf16[8,128,256]{2,1,0:T(8,128)(2,1)}), bf16[8,128,256]{2,1,0:T(8,128)(2,1)S(1)}, u32[]{:S(2)}, u32[]{:S(2)}) async-start(bf16[8,128,256]{2,1,0:T(8,128)(2,1)} %bitcast.18), calls=%async_computation.3 | async-start | bytes 1048576 | tf_op jit(solution)/shard_map/all_to_all | solution.py:89
  47.2 13.9 %all-to-all-done.3 = bf16[8,128,256]{2,1,0:T(8,128)(2,1)S(1)} async-done(((bf16[8,128,256]{2,1,0:T(8,128)(2,1)}), bf16[8,128,256]{2,1,0:T(8,128)(2,1)S(1)}, u32[]{:S(2)}, u32[]{:S(2)}) %all-to-all-start.3) | async-done | bytes 524320 | tf_op jit(solution)/shard_map/all_to_all | solution.py:89
  63.1 2.8 %add_convert_fusion.6 = (bf16[1,8,128,256]{3,2,1,0:T(8,128)(2,1)S(1)}, bf16[1,8,128,256]{3,2,1,0:T(8,128)(2,1)S(1)}, bf16[1,8,128,256]{3,2,1,0:T(8,128)(2,1)S(1)...) fusion(f32[1,8,128,256]{3,1,2,0:T(8,128)S(1)} %bitcast.62, ...), kind=kLoop, calls=%fused_computation.50 | loop fusion | flops 6291456 | bytes 9453568 | tf_op jit(solution)/shard_map/convert.6
  65.9 1.1 pad_maximum_fusion
  66.9 1.1 pad_maximum_fusion.1
  68.5 2.5 %fusion.36 = (bf16[256,256]{1,0:T(8,128)(2,1)S(1)}, bf16[256,256]{1,0:T(8,128)(2,1)S(1)}, bf16[256,256]{1,0:T(8,128)(2,1)S(1)}, bf16[256,256]{1,0:T(8,128)(2,1)S...) fusion(s32[256]{0:T(256)S(1)} %multiply_add_fusion.1), kind=kLoop, calls=%fused_computation.85 | loop fusion | flops 2359296 | bytes 787456 | tf_op jit(solution)/shard_map/convert.15
  71.2 1.5 %add_convert_fusion.2 = bf16[2,8,128,256]{3,2,1,0:T(8,128)(2,1)S(1)} fusion(bf16[2,8,128,256]{3,2,1,0:T(8,128)(2,1)} %collective-permute-done, f32[]{:T(128)S(6)} %convert_element_type.121, bf16[1,8,128,256]{3,2,1,0:T(8,128)(2,1)S(1)} %get-tuple-element.47, bf16[1,8,128,256]{3,2,1,0:T(8,128)(2,1)S(1)} %get-tuple-element.48), kind=kLoop, calls=%fused_computation.13 | loop fusion | flops 3145728 | bytes 3145732 | tf_op jit(solution)/shard_map/convert_element_type | solution.py:92
  72.9 1.5 %add_convert_fusion.1 = bf16[2,8,128,256]{3,2,1,0:T(8,128)(2,1)S(1)} fusion(bf16[2,8,128,256]{3,2,1,0:T(8,128)(2,1)} %collective-permute-done.1, f32[]{:T(128)S(6)} %convert_element_type.121, bf16[1,8,128,256]{3,2,1,0:T(8,128)(2,1)S(1)} %get-tuple-element.45, bf16[1,8,128,256]{3,2,1,0:T(8,128)(2,1)S(1)} %get-tuple-element.46), kind=kLoop, calls=%fused_computation.12 | loop fusion | flops 3145728 | bytes 3145732 | tf_op jit(solution)/shard_map/convert_element_type | solution.py:92
  77.3 1.0 multiply_add_fusion
  83.9 1.0 collective-permute-done.4
  85.4 1.1 subtract_convert_fusion
  88.5 3.7 %all-to-all-start.5 = ((bf16[8,128,256]{2,1,0:T(8,128)(2,1)}), bf16[8,128,256]{2,1,0:T(8,128)(2,1)S(1)}, u32[]{:S(2)}, u32[]{:S(2)}) async-start(bf16[8,128,256]{2,1,0:T(8,128)(2,1)} %copy.58), calls=%async_computation.5 | async-start | bytes 1048576 | tf_op jit(solution)/shard_map/all_to_all | solution.py:110
  94.1 13.1 %all-to-all-done.5 = bf16[8,128,256]{2,1,0:T(8,128)(2,1)S(1)} async-done(((bf16[8,128,256]{2,1,0:T(8,128)(2,1)}), bf16[8,128,256]{2,1,0:T(8,128)(2,1)S(1)}, u32[]{:S(2)}, u32[]{:S(2)}) %all-to-all-start.5) | async-done | bytes 524320 | tf_op jit(solution)/shard_map/all_to_all | solution.py:110
  107.2 3.6 %all-to-all-start.2 = ((bf16[8,128,256]{2,1,0:T(8,128)(2,1)}), bf16[8,128,256]{2,1,0:T(8,128)(2,1)S(1)}, u32[]{:S(2)}, u32[]{:S(2)}) async-start(bf16[8,128,256]{2,1,0:T(8,128)(2,1)} %copy.49), calls=%async_computation.2 | async-start | bytes 1048576 | tf_op jit(solution)/shard_map/all_to_all | solution.py:110
  112.8 12.7 %all-to-all-done.2 = bf16[8,128,256]{2,1,0:T(8,128)(2,1)S(1)} async-done(((bf16[8,128,256]{2,1,0:T(8,128)(2,1)}), bf16[8,128,256]{2,1,0:T(8,128)(2,1)S(1)}, u32[]{:S(2)}, u32[]{:S(2)}) %all-to-all-start.2) | async-done | bytes 524320 | tf_op jit(solution)/shard_map/all_to_all | solution.py:110
  125.5 3.6 %all-to-all-start.4 = ((bf16[8,128,256]{2,1,0:T(8,128)(2,1)}), bf16[8,128,256]{2,1,0:T(8,128)(2,1)S(1)}, u32[]{:S(2)}, u32[]{:S(2)}) async-start(bf16[8,128,256]{2,1,0:T(8,128)(2,1)} %copy.56), calls=%async_computation.4 | async-start | bytes 1048576 | tf_op jit(solution)/shard_map/all_to_all | solution.py:110
  129.2 1.0 copy.59
  131.2 12.7 %all-to-all-done.4 = bf16[8,128,256]{2,1,0:T(8,128)(2,1)S(1)} async-done(((bf16[8,128,256]{2,1,0:T(8,128)(2,1)}), bf16[8,128,256]{2,1,0:T(8,128)(2,1)S(1)}, u32[]{:S(2)}, u32[]{:S(2)}) %all-to-all-start.4) | async-done | bytes 524320 | tf_op jit(solution)/shard_map/all_to_all | solution.py:110
  143.9 1.0 copy.57
  (61 shorter events, 21.0 us)
Async XLA Ops:
  0.6 9.4 %copy-start = (bf16[256,1024]{1,0:T(8,128)(2,1)S(1)}, bf16[256,1024]{1,0:T(8,128)(2,1)}, u32[]{:S(2)}) copy-start(bf16[256,1024]{1,0:T(8,128)(2,1)} %param.4) | copy-start | bytes 1572868
  0.6 27.5 %copy-start.1 = (bf16[256,1024]{1,0:T(8,128)(2,1)S(1)}, bf16[256,1024]{1,0:T(8,128)(2,1)}, u32[]{:S(2)}) copy-start(bf16[256,1024]{1,0:T(8,128)(2,1)} %param.5) | copy-start | bytes 1572868
  2.8 21.7 %all-to-all-start.1 = ((bf16[8,128,256]{2,1,0:T(8,128)(2,1)}), bf16[8,128,256]{2,1,0:T(8,128)(2,1)S(1)}, u32[]{:S(2)}, u32[]{:S(2)}) async-start(bf16[8,128,256]{2,1,0:T(8,128)(2,1)} %bitcast.7), calls=%async_computation.1 | async-start | bytes 1048576 | tf_op jit(solution)/shard_map/all_to_all | solution.py:89
  24.5 18.3 %all-to-all-start = ((bf16[8,128,256]{2,1,0:T(8,128)(2,1)}), bf16[8,128,256]{2,1,0:T(8,128)(2,1)S(1)}, u32[]{:S(2)}, u32[]{:S(2)}) async-start(bf16[8,128,256]{2,1,0:T(8,128)(2,1)} %bitcast.1), calls=%async_computation | async-start | bytes 1048576 | tf_op jit(solution)/shard_map/all_to_all | solution.py:89
  42.8 18.3 %all-to-all-start.3 = ((bf16[8,128,256]{2,1,0:T(8,128)(2,1)}), bf16[8,128,256]{2,1,0:T(8,128)(2,1)S(1)}, u32[]{:S(2)}, u32[]{:S(2)}) async-start(bf16[8,128,256]{2,1,0:T(8,128)(2,1)} %bitcast.18), calls=%async_computation.3 | async-start | bytes 1048576 | tf_op jit(solution)/shard_map/all_to_all | solution.py:89
  66.9 4.3 %collective-permute-start = (bf16[2,8,128,256]{3,2,1,0:T(8,128)(2,1)}, bf16[2,8,128,256]{3,2,1,0:T(8,128)(2,1)}, u32[]{:S(2)}, u32[]{:S(2)}) collective-permute-start(bf16[2,8,128,256]{3,2,1,0:T(8,128)(2,1)} %pad_maximum_fusion), channel_id=1, source_target_pairs={{0,1},{1,0},{2,3},{3,2},{4,5},{5,4},{6,7},{7,6},{8,9},{9,8},{10,11... | collective-permute-start | bytes 3145736 | tf_op jit(solution)/shard_map/ppermute | solution.py:11
  68.0 4.9 %collective-permute-start.1 = (bf16[2,8,128,256]{3,2,1,0:T(8,128)(2,1)}, bf16[2,8,128,256]{3,2,1,0:T(8,128)(2,1)}, u32[]{:S(2)}, u32[]{:S(2)}) collective-permute-start(bf16[2,8,128,256]{3,2,1,0:T(8,128)(2,1)} %pad_maximum_fusion.1), channel_id=1, source_target_pairs={{0,1},{1,0},{2,3},{3,2},{4,5},{5,4},{6,7},{7,6},{8,9},{9,8},{10,11... | collective-permute-start | bytes 3145736 | tf_op jit(solution)/shard_map/ppermute | solution.py:11
  71.2 3.4 %collective-permute-start.3 = (bf16[2,8,128,256]{3,2,1,0:T(8,128)(2,1)S(1)}, bf16[2,8,128,256]{3,2,1,0:T(8,128)(2,1)S(1)}, u32[]{:S(2)}, u32[]{:S(2)}) collective-permute-start(bf16[2,8,128,256]{3,2,1,0:T(8,128)(2,1)S(1)} %pad_maximum_fusion.2), channel_id=1, source_target_pairs={{0,1},{1,0},{2,3},{3,2},{4,5},{5,4},{6,7},{7,6},{8,9},{9,8},{10,11... | collective-permute-start | bytes 3145736 | tf_op jit(solution)/shard_map/ppermute | solution.py:11
  79.1 3.2 %collective-permute-start.2 = (bf16[1024,512]{1,0:T(8,128)(2,1)S(1)}, bf16[1024,512]{1,0:T(8,128)(2,1)S(1)}, u32[]{:S(2)}, u32[]{:S(2)}) collective-permute-start(bf16[1024,512]{1,0:T(8,128)(2,1)S(1)} %convolution_convert_fusion.2), channel_id=1, source_target_pairs={{0,1},{1,0},{2,3},{3,2},{4,5},{5,4},{6,7},{7,6},{8,9},{9,8},{10,11... | collective-permute-start | bytes 3145736 | tf_op jit(solution)/shard_map/ppermute | solution.py:11
  80.4 3.0 %collective-permute-start.5 = (bf16[1024,512]{1,0:T(8,128)(2,1)S(1)}, bf16[1024,512]{1,0:T(8,128)(2,1)S(1)}, u32[]{:S(2)}, u32[]{:S(2)}) collective-permute-start(bf16[1024,512]{1,0:T(8,128)(2,1)S(1)} %convolution_convert_fusion), channel_id=1, source_target_pairs={{0,1},{1,0},{2,3},{3,2},{4,5},{5,4},{6,7},{7,6},{8,9},{9,8},{10,11... | collective-permute-start | bytes 3145736 | tf_op jit(solution)/shard_map/ppermute | solution.py:11
  81.8 3.1 %collective-permute-start.4 = (bf16[1024,512]{1,0:T(8,128)(2,1)S(1)}, bf16[1024,512]{1,0:T(8,128)(2,1)S(1)}, u32[]{:S(2)}, u32[]{:S(2)}) collective-permute-start(bf16[1024,512]{1,0:T(8,128)(2,1)S(1)} %convolution_convert_fusion.1), channel_id=1, source_target_pairs={{0,1},{1,0},{2,3},{3,2},{4,5},{5,4},{6,7},{7,6},{8,9},{9,8},{10,11... | collective-permute-start | bytes 3145736 | tf_op jit(solution)/shard_map/ppermute | solution.py:11
  88.5 18.7 %all-to-all-start.5 = ((bf16[8,128,256]{2,1,0:T(8,128)(2,1)}), bf16[8,128,256]{2,1,0:T(8,128)(2,1)S(1)}, u32[]{:S(2)}, u32[]{:S(2)}) async-start(bf16[8,128,256]{2,1,0:T(8,128)(2,1)} %copy.58), calls=%async_computation.5 | async-start | bytes 1048576 | tf_op jit(solution)/shard_map/all_to_all | solution.py:110
  107.2 18.3 %all-to-all-start.2 = ((bf16[8,128,256]{2,1,0:T(8,128)(2,1)}), bf16[8,128,256]{2,1,0:T(8,128)(2,1)S(1)}, u32[]{:S(2)}, u32[]{:S(2)}) async-start(bf16[8,128,256]{2,1,0:T(8,128)(2,1)} %copy.49), calls=%async_computation.2 | async-start | bytes 1048576 | tf_op jit(solution)/shard_map/all_to_all | solution.py:110
  125.5 18.3 %all-to-all-start.4 = ((bf16[8,128,256]{2,1,0:T(8,128)(2,1)}), bf16[8,128,256]{2,1,0:T(8,128)(2,1)S(1)}, u32[]{:S(2)}, u32[]{:S(2)}) async-start(bf16[8,128,256]{2,1,0:T(8,128)(2,1)} %copy.56), calls=%async_computation.4 | async-start | bytes 1048576 | tf_op jit(solution)/shard_map/all_to_all | solution.py:110
where the time goes:
time: 146 us; the launch traced here: 145 us
  waiting for transfers between devices  81.3 us (56%)
  starting transfers between devices  27.2 us (19%)
  other arithmetic  15 us (10%)
  local copies, waits for them, and re-layouts  13.6 us (9%)
  matrix products  6.81 us (5%)
    all_to_all x3, waiting for transfers between devices, spectrum(): lax.all_to_all(arranged, 'wide', split_axis=0, concat_axis=0, tiled=True)  41.1 us
    all_to_all x3, waiting for transfers between devices, invert(): lax.all_to_all(arranged, 'wide', split_axis=0, concat_axis=1, tiled=True)  38.5 us
    all_to_all x3, starting transfers between devices, spectrum(): lax.all_to_all(arranged, 'wide', split_axis=0, concat_axis=0, tiled=True)  14.5 us
    all_to_all x3, starting transfers between devices, invert(): lax.all_to_all(arranged, 'wide', split_axis=0, concat_axis=1, tiled=True)  10.9 us
    another operation x5, other arithmetic  6.97 us
    reshape x3, local copies, waits for them, and re-layouts, spectrum(): arranged = jnp.transpose(signal).reshape(span_count, shares, blocksize)  4.13 us
    convert_element_type x3, other arithmetic, spectrum(): (signed * twisted.astype(jnp.float32) + partner.astype(jnp.float32)).asty...  3.43 us
    reshape x3, local copies, waits for them, and re-layouts, invert(): return jnp.transpose(returned.reshape(channels, blocksize))  3 us
  transfers between devices with their start and end apart: 12, of which 8 were waited for; matrix products, arithmetic and copies ran while one was open for 13% of the time, Pallas kernels for 0%

commit v1 on v0

--- a/solution.py
+++ b/solution.py
@@ -107,7 +107,12 @@
         comb_re = combined[:, :blocksize].reshape(span_count, shares, blocksize)
         comb_im = combined[:, blocksize:].reshape(span_count, shares, blocksize)
         arranged = long_back(comb_re, comb_im, twist_cos, twist_sin)
-        returned = lax.all_to_all(arranged, "wide", split_axis=0, concat_axis=1, tiled=True)
+        returned = jnp.concatenate(
+            lax.all_to_all(
+                jnp.stack(jnp.split(arranged, lax.axis_size("wide"), axis=0)), "wide", 0, 0
+            ),
+            axis=1,
+        )
         return jnp.transpose(returned.reshape(channels, blocksize))
 
     def product(left_side, right_side, conjugate, factor):

time: 146 us -> 153 us (1.048)
  local copies, waits for them, and re-layouts: 13.6 us -> 35.3 us
  waiting for transfers between devices: 81.3 us -> 66.8 us
    all_to_all x3, waiting for transfers between devices: 38.5 us -> 24.1 us  [invert(): lax.all_to_all(jnp.stack(jnp.split(arranged, lax.axis_size('wide'), axis=...]
    unnamed x10 -> x31, local copies, waits for them, and re-layouts: 2.65 us -> 16 us
    split x0 -> x3, local copies, waits for them, and re-layouts: none -> 8.54 us  [invert(): jnp.split(arranged, lax.axis_size('wide'), axis=0)]
    reshape x6 -> x0, local copies, waits for them, and re-layouts: 5.69 us -> none  [the longest x3 3 us: invert(): return jnp.transpose(returned.reshape(channels, blocksize))]
    another operation x0 -> x30, local copies, waits for them, and re-layouts: none -> 5.55 us  [the longest x3 3 us: invert(): return jnp.transpose(returned.reshape(channels, blocksize))]
  transfers between devices with their start and end apart: 12 -> 12, of which waited for: 8 -> 8; matrix products, arithmetic and copies ran while one was open for 13% -> 22% of each run, Pallas kernels for 0% -> 0%
where the time goes in v1:
time: 153 us; the launch traced here: 152 us
  waiting for transfers between devices  66.8 us (44%)
  local copies, waits for them, and re-layouts  35.3 us (23%)
  starting transfers between devices  27.2 us (18%)
  other arithmetic  15 us (10%)
  matrix products  6.81 us (4%)
    all_to_all x3, waiting for transfers between devices, spectrum(): lax.all_to_all(arranged, 'wide', split_axis=0, concat_axis=0, tiled=True)  41.1 us
    all_to_all x3, waiting for transfers between devices, invert(): lax.all_to_all(jnp.stack(jnp.split(arranged, lax.axis_size('wide'), axis=...  24.1 us
    unnamed x31, local copies, waits for them, and re-layouts  16 us
    all_to_all x3, starting transfers between devices, spectrum(): lax.all_to_all(arranged, 'wide', split_axis=0, concat_axis=0, tiled=True)  14.5 us
    all_to_all x3, starting transfers between devices, invert(): lax.all_to_all(jnp.stack(jnp.split(arranged, lax.axis_size('wide'), axis=...  10.9 us
    split x3, local copies, waits for them, and re-layouts, invert(): jnp.split(arranged, lax.axis_size('wide'), axis=0)  8.54 us
    another operation x5, other arithmetic  6.97 us
    reshape x3, local copies, waits for them, and re-layouts, spectrum(): arranged = jnp.transpose(signal).reshape(span_count, shares, blocksize)  4.13 us
  transfers between devices with their start and end apart: 12, of which 8 were waited for; matrix products, arithmetic and copies ran while one was open for 22% of the time, Pallas kernels for 0%

profile of v1, /device:TPU:0, one launch (start us, length us, event | category | flops | bytes accessed | tf_op | source)
XLA Modules:
  0.0 152.3 jit_solution(13159694186192850210)
XLA Ops:
  0.7 2.1 %copy.40 = bf16[1024,256]{1,0:T(8,128)(2,1)} copy(bf16[1024,256]{0,1:T(8,128)(2,1)} %bitcast.78) | data formatting | bytes 1048576 | tf_op jit(solution)/shard_map/reshape | solution.py:87
  2.8 7.3 %all-to-all-start.1 = ((bf16[8,128,256]{2,1,0:T(8,128)(2,1)}), bf16[8,128,256]{2,1,0:T(8,128)(2,1)S(1)}, u32[]{:S(2)}, u32[]{:S(2)}) async-start(bf16[8,128,256]{2,1,0:T(8,128)(2,1)} %bitcast.7), calls=%async_computation.1 | async-start | bytes 1048576 | tf_op jit(solution)/shard_map/all_to_all | solution.py:89
  11.0 13.5 %all-to-all-done.1 = bf16[8,128,256]{2,1,0:T(8,128)(2,1)S(1)} async-done(((bf16[8,128,256]{2,1,0:T(8,128)(2,1)}), bf16[8,128,256]{2,1,0:T(8,128)(2,1)S(1)}, u32[]{:S(2)}, u32[]{:S(2)}) %all-to-all-start.1) | async-done | bytes 524320 | tf_op jit(solution)/shard_map/all_to_all | solution.py:89
  24.5 3.6 %all-to-all-start = ((bf16[8,128,256]{2,1,0:T(8,128)(2,1)}), bf16[8,128,256]{2,1,0:T(8,128)(2,1)S(1)}, u32[]{:S(2)}, u32[]{:S(2)}) async-start(bf16[8,128,256]{2,1,0:T(8,128)(2,1)} %bitcast.1), calls=%async_computation | async-start | bytes 1048576 | tf_op jit(solution)/shard_map/all_to_all | solution.py:89
  29.2 13.7 %all-to-all-done = bf16[8,128,256]{2,1,0:T(8,128)(2,1)S(1)} async-done(((bf16[8,128,256]{2,1,0:T(8,128)(2,1)}), bf16[8,128,256]{2,1,0:T(8,128)(2,1)S(1)}, u32[]{:S(2)}, u32[]{:S(2)}) %all-to-all-start) | async-done | bytes 524320 | tf_op jit(solution)/shard_map/all_to_all | solution.py:89
  42.8 3.6 %all-to-all-start.3 = ((bf16[8,128,256]{2,1,0:T(8,128)(2,1)}), bf16[8,128,256]{2,1,0:T(8,128)(2,1)S(1)}, u32[]{:S(2)}, u32[]{:S(2)}) async-start(bf16[8,128,256]{2,1,0:T(8,128)(2,1)} %bitcast.17), calls=%async_computation.3 | async-start | bytes 1048576 | tf_op jit(solution)/shard_map/all_to_all | solution.py:89
  47.2 13.9 %all-to-all-done.3 = bf16[8,128,256]{2,1,0:T(8,128)(2,1)S(1)} async-done(((bf16[8,128,256]{2,1,0:T(8,128)(2,1)}), bf16[8,128,256]{2,1,0:T(8,128)(2,1)S(1)}, u32[]{:S(2)}, u32[]{:S(2)}) %all-to-all-start.3) | async-done | bytes 524320 | tf_op jit(solution)/shard_map/all_to_all | solution.py:89
  63.1 2.8 %add_convert_fusion.6 = (bf16[1,8,128,256]{3,2,1,0:T(8,128)(2,1)S(1)}, bf16[1,8,128,256]{3,2,1,0:T(8,128)(2,1)S(1)}, bf16[1,8,128,256]{3,2,1,0:T(8,128)(2,1)S(1)...) fusion(f32[1,8,128,256]{3,1,2,0:T(8,128)S(1)} %bitcast.59, ...), kind=kLoop, calls=%fused_computation.50 | loop fusion | flops 6291456 | bytes 9453568 | tf_op jit(solution)/shard_map/convert.6
  65.9 1.1 pad_maximum_fusion
  66.9 1.1 pad_maximum_fusion.1
  68.5 2.5 %fusion.36 = (bf16[256,256]{1,0:T(8,128)(2,1)S(1)}, bf16[256,256]{1,0:T(8,128)(2,1)S(1)}, bf16[256,256]{1,0:T(8,128)(2,1)S(1)}, bf16[256,256]{1,0:T(8,128)(2,1)S...) fusion(s32[256]{0:T(256)S(1)} %multiply_add_fusion.1), kind=kLoop, calls=%fused_computation.109 | loop fusion | flops 2359296 | bytes 787456 | tf_op jit(solution)/shard_map/convert.15
  71.2 1.5 %add_convert_fusion.2 = bf16[2,8,128,256]{3,2,1,0:T(8,128)(2,1)S(1)} fusion(bf16[2,8,128,256]{3,2,1,0:T(8,128)(2,1)} %collective-permute-done, f32[]{:T(128)S(6)} %convert_element_type.121, bf16[1,8,128,256]{3,2,1,0:T(8,128)(2,1)S(1)} %get-tuple-element.71, bf16[1,8,128,256]{3,2,1,0:T(8,128)(2,1)S(1)} %get-tuple-element.72), kind=kLoop, calls=%fused_computation.13 | loop fusion | flops 3145728 | bytes 3145732 | tf_op jit(solution)/shard_map/convert_element_type | solution.py:92
  72.9 1.5 %add_convert_fusion.1 = bf16[2,8,128,256]{3,2,1,0:T(8,128)(2,1)S(1)} fusion(bf16[2,8,128,256]{3,2,1,0:T(8,128)(2,1)} %collective-permute-done.1, f32[]{:T(128)S(6)} %convert_element_type.121, bf16[1,8,128,256]{3,2,1,0:T(8,128)(2,1)S(1)} %get-tuple-element.69, bf16[1,8,128,256]{3,2,1,0:T(8,128)(2,1)S(1)} %get-tuple-element.70), kind=kLoop, calls=%fused_computation.12 | loop fusion | flops 3145728 | bytes 3145732 | tf_op jit(solution)/shard_map/convert_element_type | solution.py:92
  77.3 1.0 multiply_add_fusion
  85.4 1.1 subtract_convert_fusion
  87.6 3.0 %slice_reduce_fusion = (bf16[32768]{0:T(1024)(128)(2,1)S(1)}, bf16[32768]{0:T(1024)(128)(2,1)S(1)}, bf16[32768]{0:T(1024)(128)(2,1)S(1)}, bf16[32768]{0:T(1024)(...) fusion(bf16[8,32768]{1,0:T(8,128)(2,1)S(1)} %fusion.2), kind=kLoop, calls=%fused_computation.84 | loop fusion | bytes 1048576 | tf_op jit(solution)/shard_map/split | solution.py:112
  96.0 3.7 %all-to-all-start.5 = ((bf16[8,1,128,256]{3,2,1,0:T(8,128)(2,1)}), bf16[8,1,128,256]{3,2,1,0:T(8,128)(2,1)S(1)}, u32[]{:S(2)}, u32[]{:S(2)}) async-start(bf16[8,1,128,256]{3,2,1,0:T(8,128)(2,1)} %constant_dynamic-update-slice_fusion.16), calls=%async_computation.5 | async-start | bytes 1048576 | tf_op jit(solution)/shard_map/all_to_all | solution.py:111
  100.7 2.8 %slice_reduce_fusion.16 = (bf16[32768]{0:T(1024)(128)(2,1)S(1)}, bf16[32768]{0:T(1024)(128)(2,1)S(1)}, bf16[32768]{0:T(1024)(128)(2,1)S(1)}, bf16[32768]{0:T(102...) fusion(bf16[8,32768]{1,0:T(8,128)(2,1)S(1)} %fusion), kind=kLoop, calls=%fused_computation.100 | loop fusion | bytes 1048576 | tf_op jit(solution)/shard_map/split | solution.py:112
  109.9 4.8 %all-to-all-done.5 = bf16[8,1,128,256]{3,2,1,0:T(8,128)(2,1)S(1)} async-done(((bf16[8,1,128,256]{3,2,1,0:T(8,128)(2,1)}), bf16[8,1,128,256]{3,2,1,0:T(8,128)(2,1)S(1)}, u32[]{:S(2)}, u32[]{:S(2)}) %all-to-all-start.5) | async-done | bytes 524320 | tf_op jit(solution)/shard_map/all_to_all | solution.py:111
  114.7 3.6 %all-to-all-start.2 = ((bf16[8,1,128,256]{3,2,1,0:T(8,128)(2,1)}), bf16[8,1,128,256]{3,2,1,0:T(8,128)(2,1)S(1)}, u32[]{:S(2)}, u32[]{:S(2)}) async-start(bf16[8,1,128,256]{3,2,1,0:T(8,128)(2,1)} %constant_dynamic-update-slice_fusion), calls=%async_computation.2 | async-start | bytes 1048576 | tf_op jit(solution)/shard_map/all_to_all | solution.py:111
  118.3 2.8 %slice_reduce_fusion.8 = (bf16[32768]{0:T(1024)(128)(2,1)S(1)}, bf16[32768]{0:T(1024)(128)(2,1)S(1)}, bf16[32768]{0:T(1024)(128)(2,1)S(1)}, bf16[32768]{0:T(1024...) fusion(bf16[8,32768]{1,0:T(8,128)(2,1)S(1)} %fusion.1), kind=kLoop, calls=%fused_computation.92 | loop fusion | bytes 1048576 | tf_op jit(solution)/shard_map/split | solution.py:112
  126.5 6.6 %all-to-all-done.2 = bf16[8,1,128,256]{3,2,1,0:T(8,128)(2,1)S(1)} async-done(((bf16[8,1,128,256]{3,2,1,0:T(8,128)(2,1)}), bf16[8,1,128,256]{3,2,1,0:T(8,128)(2,1)S(1)}, u32[]{:S(2)}, u32[]{:S(2)}) %all-to-all-start.2) | async-done | bytes 524320 | tf_op jit(solution)/shard_map/all_to_all | solution.py:111
  133.0 3.6 %all-to-all-start.4 = ((bf16[8,1,128,256]{3,2,1,0:T(8,128)(2,1)}), bf16[8,1,128,256]{3,2,1,0:T(8,128)(2,1)S(1)}, u32[]{:S(2)}, u32[]{:S(2)}) async-start(bf16[8,1,128,256]{3,2,1,0:T(8,128)(2,1)} %constant_dynamic-update-slice_fusion.8), calls=%async_computation.4 | async-start | bytes 1048576 | tf_op jit(solution)/shard_map/all_to_all | solution.py:111
  138.7 12.7 %all-to-all-done.4 = bf16[8,1,128,256]{3,2,1,0:T(8,128)(2,1)S(1)} async-done(((bf16[8,1,128,256]{3,2,1,0:T(8,128)(2,1)}), bf16[8,1,128,256]{3,2,1,0:T(8,128)(2,1)S(1)}, u32[]{:S(2)}, u32[]{:S(2)}) %all-to-all-start.4) | async-done | bytes 524320 | tf_op jit(solution)/shard_map/all_to_all | solution.py:111
  (109 shorter events, 37.2 us)
Async XLA Ops:
  0.6 9.4 %copy-start = (bf16[256,1024]{1,0:T(8,128)(2,1)S(1)}, bf16[256,1024]{1,0:T(8,128)(2,1)}, u32[]{:S(2)}) copy-start(bf16[256,1024]{1,0:T(8,128)(2,1)} %param.4) | copy-start | bytes 1572868
  0.6 27.5 %copy-start.1 = (bf16[256,1024]{1,0:T(8,128)(2,1)S(1)}, bf16[256,1024]{1,0:T(8,128)(2,1)}, u32[]{:S(2)}) copy-start(bf16[256,1024]{1,0:T(8,128)(2,1)} %param.5) | copy-start | bytes 1572868
  2.8 21.7 %all-to-all-start.1 = ((bf16[8,128,256]{2,1,0:T(8,128)(2,1)}), bf16[8,128,256]{2,1,0:T(8,128)(2,1)S(1)}, u32[]{:S(2)}, u32[]{:S(2)}) async-start(bf16[8,128,256]{2,1,0:T(8,128)(2,1)} %bitcast.7), calls=%async_computation.1 | async-start | bytes 1048576 | tf_op jit(solution)/shard_map/all_to_all | solution.py:89
  24.5 18.3 %all-to-all-start = ((bf16[8,128,256]{2,1,0:T(8,128)(2,1)}), bf16[8,128,256]{2,1,0:T(8,128)(2,1)S(1)}, u32[]{:S(2)}, u32[]{:S(2)}) async-start(bf16[8,128,256]{2,1,0:T(8,128)(2,1)} %bitcast.1), calls=%async_computation | async-start | bytes 1048576 | tf_op jit(solution)/shard_map/all_to_all | solution.py:89
  42.8 18.3 %all-to-all-start.3 = ((bf16[8,128,256]{2,1,0:T(8,128)(2,1)}), bf16[8,128,256]{2,1,0:T(8,128)(2,1)S(1)}, u32[]{:S(2)}, u32[]{:S(2)}) async-start(bf16[8,128,256]{2,1,0:T(8,128)(2,1)} %bitcast.17), calls=%async_computation.3 | async-start | bytes 1048576 | tf_op jit(solution)/shard_map/all_to_all | solution.py:89
  66.9 4.3 %collective-permute-start = (bf16[2,8,128,256]{3,2,1,0:T(8,128)(2,1)}, bf16[2,8,128,256]{3,2,1,0:T(8,128)(2,1)}, u32[]{:S(2)}, u32[]{:S(2)}) collective-permute-start(bf16[2,8,128,256]{3,2,1,0:T(8,128)(2,1)} %pad_maximum_fusion), channel_id=1, source_target_pairs={{0,1},{1,0},{2,3},{3,2},{4,5},{5,4},{6,7},{7,6},{8,9},{9,8},{10,11... | collective-permute-start | bytes 3145736 | tf_op jit(solution)/shard_map/ppermute | solution.py:11
  68.0 4.9 %collective-permute-start.1 = (bf16[2,8,128,256]{3,2,1,0:T(8,128)(2,1)}, bf16[2,8,128,256]{3,2,1,0:T(8,128)(2,1)}, u32[]{:S(2)}, u32[]{:S(2)}) collective-permute-start(bf16[2,8,128,256]{3,2,1,0:T(8,128)(2,1)} %pad_maximum_fusion.1), channel_id=1, source_target_pairs={{0,1},{1,0},{2,3},{3,2},{4,5},{5,4},{6,7},{7,6},{8,9},{9,8},{10,11... | collective-permute-start | bytes 3145736 | tf_op jit(solution)/shard_map/ppermute | solution.py:11
  71.2 3.4 %collective-permute-start.3 = (bf16[2,8,128,256]{3,2,1,0:T(8,128)(2,1)S(1)}, bf16[2,8,128,256]{3,2,1,0:T(8,128)(2,1)S(1)}, u32[]{:S(2)}, u32[]{:S(2)}) collective-permute-start(bf16[2,8,128,256]{3,2,1,0:T(8,128)(2,1)S(1)} %pad_maximum_fusion.2), channel_id=1, source_target_pairs={{0,1},{1,0},{2,3},{3,2},{4,5},{5,4},{6,7},{7,6},{8,9},{9,8},{10,11... | collective-permute-start | bytes 3145736 | tf_op jit(solution)/shard_map/ppermute | solution.py:11
  79.1 3.2 %collective-permute-start.2 = (bf16[1024,512]{1,0:T(8,128)(2,1)S(1)}, bf16[1024,512]{1,0:T(8,128)(2,1)S(1)}, u32[]{:S(2)}, u32[]{:S(2)}) collective-permute-start(bf16[1024,512]{1,0:T(8,128)(2,1)S(1)} %convolution_convert_fusion.2), channel_id=1, source_target_pairs={{0,1},{1,0},{2,3},{3,2},{4,5},{5,4},{6,7},{7,6},{8,9},{9,8},{10,11... | collective-permute-start | bytes 3145736 | tf_op jit(solution)/shard_map/ppermute | solution.py:11
  80.4 3.0 %collective-permute-start.5 = (bf16[1024,512]{1,0:T(8,128)(2,1)S(1)}, bf16[1024,512]{1,0:T(8,128)(2,1)S(1)}, u32[]{:S(2)}, u32[]{:S(2)}) collective-permute-start(bf16[1024,512]{1,0:T(8,128)(2,1)S(1)} %convolution_convert_fusion), channel_id=1, source_target_pairs={{0,1},{1,0},{2,3},{3,2},{4,5},{5,4},{6,7},{7,6},{8,9},{9,8},{10,11... | collective-permute-start | bytes 3145736 | tf_op jit(solution)/shard_map/ppermute | solution.py:11
  81.8 3.1 %collective-permute-start.4 = (bf16[1024,512]{1,0:T(8,128)(2,1)S(1)}, bf16[1024,512]{1,0:T(8,128)(2,1)S(1)}, u32[]{:S(2)}, u32[]{:S(2)}) collective-permute-start(bf16[1024,512]{1,0:T(8,128)(2,1)S(1)} %convolution_convert_fusion.1), channel_id=1, source_target_pairs={{0,1},{1,0},{2,3},{3,2},{4,5},{5,4},{6,7},{7,6},{8,9},{9,8},{10,11... | collective-permute-start | bytes 3145736 | tf_op jit(solution)/shard_map/ppermute | solution.py:11
  96.0 18.7 %all-to-all-start.5 = ((bf16[8,1,128,256]{3,2,1,0:T(8,128)(2,1)}), bf16[8,1,128,256]{3,2,1,0:T(8,128)(2,1)S(1)}, u32[]{:S(2)}, u32[]{:S(2)}) async-start(bf16[8,1,128,256]{3,2,1,0:T(8,128)(2,1)} %constant_dynamic-update-slice_fusion.16), calls=%async_computation.5 | async-start | bytes 1048576 | tf_op jit(solution)/shard_map/all_to_all | solution.py:111
  114.7 18.3 %all-to-all-start.2 = ((bf16[8,1,128,256]{3,2,1,0:T(8,128)(2,1)}), bf16[8,1,128,256]{3,2,1,0:T(8,128)(2,1)S(1)}, u32[]{:S(2)}, u32[]{:S(2)}) async-start(bf16[8,1,128,256]{3,2,1,0:T(8,128)(2,1)} %constant_dynamic-update-slice_fusion), calls=%async_computation.2 | async-start | bytes 1048576 | tf_op jit(solution)/shard_map/all_to_all | solution.py:111
  133.0 18.3 %all-to-all-start.4 = ((bf16[8,1,128,256]{3,2,1,0:T(8,128)(2,1)}), bf16[8,1,128,256]{3,2,1,0:T(8,128)(2,1)S(1)}, u32[]{:S(2)}, u32[]{:S(2)}) async-start(bf16[8,1,128,256]{3,2,1,0:T(8,128)(2,1)} %constant_dynamic-update-slice_fusion.8), calls=%async_computation.4 | async-start | bytes 1048576 | tf_op jit(solution)/shard_map/all_to_all | solution.py:111
